TPU v7x, 32 devices: a whole 2x2x4 slice. The times are simulated.
32 devices in a mesh: clip: 2 (over x), gx: 8 (over z, y), gy: 2 (over core).
Axes of the slice: x: 2, y: 2, z: 4, core: 2. Of those that a mesh axis runs over, the one named last changes fastest.
Arguments:
- e_field: float32 [3, 128, 128, 128], P(None, ('clip', 'gx'), 'gy'), parts along dimension 1, may hold values from -6 to 6
- h_field: float32 [3, 128, 128, 128], P(None, ('clip', 'gx'), 'gy'), parts along dimension 1, may hold values from -6 to 6
- material: int32 [128, 128, 128], P(('clip', 'gx'), 'gy'), parts along dimension 0, may hold values from 0 to 5
- eps_table: float32 [6], replicated, may hold values from 0.8 to 1.2
- sigma_table: float32 [6], replicated, may hold values from 0 to 2
- angle_orders: int32 [64, 2], replicated, may hold values from -8 to 8
Outputs:
- e_out: float32 [3, 128, 128, 128], P(None, ('clip', 'gx'), 'gy'), parts along dimension 1
- h_out: float32 [3, 128, 128, 128], P(None, ('clip', 'gx'), 'gy'), parts along dimension 1
- far_field: float32 [128, 4], P(('clip', 'gx')), parts along dimension 0
There are 2 independent parts, one for each index of `clip`. A program takes and returns all parts, laid end to end along the dimension named above; an argument that names none is the same for every part. Nothing has to cross between parts.
All inputs are finite; a program needn't handle non-finite values.
Results may differ from a plain program's by a relative error of at most 0.00021.
Values sent between devices are 32-bit elements; how exact they have to be, the bound alone decides.
A program may use at most 64 MiB of HBM per device.

v0:
```python
import math

import jax
import jax.numpy as jnp
from jax import lax
from jax.sharding import PartitionSpec as P

ITERS = 4


TIME_STEP = 0.5
PHASE_STEP = 0.9


def shifted(value, axis, steps):
    count = lax.axis_size(axis)
    pairs = [(source, (source + steps) % count) for source in range(count)]
    return lax.ppermute(value, axis, pairs)


def forward_z(field):
    upper = jnp.concatenate([field[..., 1:], jnp.zeros_like(field[..., :1])], axis=-1)
    return upper - field


def backward_z(field):
    lower = jnp.concatenate([jnp.zeros_like(field[..., :1]), field[..., :-1]], axis=-1)
    return field - lower


def coefficients(material, eps_table, sigma_table):
    count = eps_table.shape[0]
    labels = jnp.arange(count, dtype=jnp.int32).reshape(count, 1, 1, 1)
    onehot = (material[None] == labels).astype(jnp.float32)
    permit = jnp.sum(onehot * eps_table.reshape(count, 1, 1, 1), axis=0)
    conduct = jnp.sum(onehot * sigma_table.reshape(count, 1, 1, 1), axis=0)
    loss = conduct * TIME_STEP / (2.0 * permit)
    keep = (1.0 - loss) / (1.0 + loss)
    drive = TIME_STEP / (permit * (1.0 + loss))
    return (keep, drive)


def split_step(elec, magn, keep, drive):
    ahead_x = shifted(elec[1:3, 0:1], "gx", -1)
    ahead_y = shifted(jnp.stack([elec[0, :, 0:1], elec[2, :, 0:1]]), "gy", -1)
    ext_x = jnp.concatenate([elec[1:3], ahead_x], axis=1)
    diff_x = ext_x[:, 1:] - ext_x[:, :-1]
    ext_y = jnp.concatenate([jnp.stack([elec[0], elec[2]]), ahead_y], axis=2)
    diff_y = ext_y[:, :, 1:] - ext_y[:, :, :-1]
    magn_x = magn[0] - TIME_STEP * (diff_y[1] - forward_z(elec[1]))
    magn_y = magn[1] - TIME_STEP * (forward_z(elec[0]) - diff_x[1])
    magn_z = magn[2] - TIME_STEP * (diff_x[0] - diff_y[0])
    magn = jnp.stack([magn_x, magn_y, magn_z])
    behind_x = shifted(magn[1:3, -1:], "gx", 1)
    behind_y = shifted(jnp.stack([magn[0, :, -1:], magn[2, :, -1:]]), "gy", 1)
    back_x = jnp.concatenate([behind_x, magn[1:3]], axis=1)
    bdiff_x = back_x[:, 1:] - back_x[:, :-1]
    back_y = jnp.concatenate([behind_y, jnp.stack([magn[0], magn[2]])], axis=2)
    bdiff_y = back_y[:, :, 1:] - back_y[:, :, :-1]
    elec_x = keep * elec[0] + drive * (bdiff_y[1] - backward_z(magn[1]))
    elec_y = keep * elec[1] + drive * (backward_z(magn[0]) - bdiff_x[1])
    elec_z = keep * elec[2] + drive * (bdiff_x[0] - bdiff_y[0])
    return (jnp.stack([elec_x, elec_y, elec_z]), magn)


def local(e_field, h_field, material, eps_table, sigma_table, angle_orders):
    keep, drive = coefficients(material, eps_table, sigma_table)
    cells_x = e_field.shape[1]
    cells_y = e_field.shape[2]
    depth = e_field.shape[3]
    elec = e_field
    magn = h_field
    mon_real = jnp.zeros((2, cells_x, cells_y), jnp.float32)
    mon_imag = jnp.zeros((2, cells_x, cells_y), jnp.float32)
    for number in range(ITERS):
        elec, magn = split_step(elec, magn, keep, drive)
        plane = elec[0:2, :, :, depth - 3]
        mon_real = mon_real + math.cos(PHASE_STEP * (number + 1)) * plane
        mon_imag = mon_imag - math.sin(PHASE_STEP * (number + 1)) * plane
    size_x = lax.axis_size("gx")
    size_y = lax.axis_size("gy")
    total_x = cells_x * size_x
    total_y = cells_y * size_y
    pos_x = lax.axis_index("gx") * cells_x + jnp.arange(cells_x, dtype=jnp.int32)
    pos_y = lax.axis_index("gy") * cells_y + jnp.arange(cells_y, dtype=jnp.int32)
    flat_real = mon_real.reshape(2, cells_x * cells_y).T
    flat_imag = mon_imag.reshape(2, cells_x * cells_y).T
    high = lax.Precision.HIGHEST
    angle_count = angle_orders.shape[0]
    owned = angle_count // size_x
    scale = 1.0 / math.sqrt(total_x * total_y)
    order_x = angle_orders[:, 0]
    order_y = angle_orders[:, 1]
    phase_int = (
        order_x[:, None, None] * pos_x[None, :, None] * total_y
        + order_y[:, None, None] * pos_y[None, None, :] * total_x
    ) % (total_x * total_y)
    theta = phase_int.astype(jnp.float32) * (2.0 * math.pi / (total_x * total_y))
    cosine = jnp.cos(theta).reshape(owned * lax.axis_size("gx"), cells_x * cells_y)
    sine = jnp.sin(theta).reshape(owned * lax.axis_size("gx"), cells_x * cells_y)
    real_part = jnp.dot(
        cosine, flat_real, precision=high, preferred_element_type=jnp.float32
    ) + jnp.dot(sine, flat_imag, precision=high, preferred_element_type=jnp.float32)
    imag_part = jnp.dot(
        cosine, flat_imag, precision=high, preferred_element_type=jnp.float32
    ) - jnp.dot(sine, flat_real, precision=high, preferred_element_type=jnp.float32)
    rows_sum = lax.psum_scatter(
        jnp.stack([real_part[:, 0], imag_part[:, 0], real_part[:, 1], imag_part[:, 1]], axis=1),
        "gx",
        scatter_dimension=0,
        tiled=True,
    )
    far_field = lax.psum(rows_sum, "gy") * scale
    return (elec, magn, far_field)


def solution(mesh):
    return jax.shard_map(
        local,
        mesh=mesh,
        in_specs=(
            P(None, ("clip", "gx"), "gy", None),
            P(None, ("clip", "gx"), "gy", None),
            P(("clip", "gx"), "gy", None),
            P(),
            P(),
            P(),
        ),
        out_specs=(
            P(None, ("clip", "gx"), "gy", None),
            P(None, ("clip", "gx"), "gy", None),
            P(("clip", "gx"), None),
        ),
        check_vma=False,
    )
```

profile of v0, /device:TPU:0, one launch (start us, length us, event | category | flops | bytes accessed | tf_op | source)
XLA Modules:
  0.0 148.8 jit_solution(9321898635787207260)
XLA Ops:
  3.0 5.6 %collective-permute-start.1 = (f32[2,1,64,128]{2,1,3,0:T(1,128)S(1)}, f32[2,1,64,128]{2,1,3,0:T(1,128)S(1)}, u32[]{:S(2)}, u32[]{:S(2)}) collective-permute-start(f32[2,1,64,128]{2,1,3,0:T(1,128)S(1)} %copy.141), channel_id=1, source_target_pairs={{0,14},{2,0},{4,2},{6,4},{8,6},{10,8},{12,10},{14,12},{1,15},{3,1}... | collective-permute-start | bytes 196616 | tf_op jit(solution)/shard_map/ppermute | solution.py:18
  18.9 2.0 %fusion.16 = f32[2,8,64,128]{2,1,3,0:T(8,128)S(1)} fusion(f32[2,8,64,128]{2,1,3,0:T(8,128)} %copy.180, f32[2,1,64,128]{2,1,3,0:T(1,128)S(1)} %collective-permute-done.1), kind=kLoop, calls=%fused_computation.82 | loop fusion | flops 262144 | bytes 1114112 | tf_op jit(solution)/shard_map/sub | solution.py:47
  29.1 2.4 %collective-permute-done.3 = f32[2,1,64,128]{2,1,3,0:T(1,128)S(1)} collective-permute-done((f32[2,1,64,128]{2,1,3,0:T(1,128)}, f32[2,1,64,128]{2,1,3,0:T(1,128)S(1)}, u32[]{:S(2)}, u32[]{:S(2)}) %collective-permute-start.3) | collective-permute-done | bytes 65568 | tf_op jit(solution)/shard_map/ppermute | solution.py:18
  31.5 1.7 %fusion.15 = (f32[2,8,64,128]{2,1,3,0:T(8,128)S(1)}, f32[2,8,64,128]{2,1,3,0:T(8,128)S(1)}) fusion(f32[1,8,64,128]{2,1,3,0:T(8,128)S(1)} %fusion.80, f32[1,8,64,128]{2,1,3,0:T(8,128)S(1)} %bitcast.241, f32[2,1,64,128]{2,1,3,0:T(1,128)S(1)} %collective-permute-done.3, f32[1,8,64,128]{2,1,3,0:T(8,128)S(1)} %bitcast.239, f32[2,8,1,128]{2,1,3,0:T(8,128)} %copy.144), kind=kLoop, calls=%fused_computation.52 | loop fusion | flops 1048576 | bytes 1908736 | tf_op jit(solution)/shard_map/sub | solution.py:57
  35.2 1.6 %fusion.67 = (f32[8,64,128]{1,0,2:T(8,128)S(1)}, f32[8,64,128]{1,0,2:T(8,128)S(1)}, f32[8,64,128]{1,0,2:T(8,128)S(1)}) fusion(f32[2,8,64,128]{2,1,3,0:T(8,128)S(1)} %get-tuple-element.51, f32[8,64,128]{1,0,2:T(8,128)S(1)} %fusion.83, f32[8,64,127]{1,0,2:T(8,128)S(1)} %copy-done.59, f32[1,8,64,128]{2,1,3,0:T(8,128)S(1)} %copy-done.45, ...), kind=kLoop, calls=%fused_computation.153 | loop fusion | flops 851968 | bytes 2357248 | tf_op jit(solution)/shard_map/add | solution.py:61
  36.9 2.3 %collective-permute-start.5 = (f32[2,1,64,128]{2,1,3,0:T(1,128)S(1)}, f32[2,1,64,128]{2,1,3,0:T(1,128)S(1)}, u32[]{:S(2)}, u32[]{:S(2)}) collective-permute-start(f32[2,1,64,128]{2,1,3,0:T(1,128)S(1)} %fusion.94), channel_id=1, source_target_pairs={{0,14},{2,0},{4,2},{6,4},{8,6},{10,8},{12,10},{14,12},{1,15},{3,1}... | collective-permute-start | bytes 196616 | tf_op jit(solution)/shard_map/ppermute | solution.py:18
  39.4 1.5 %fusion.78 = f32[8,64,128]{1,0,2:T(8,128)S(1)} fusion(f32[8,64,128]{1,0,2:T(8,128)S(1)} %get-tuple-element.21, f32[2,8,64,128]{2,1,3,0:T(8,128)} %copy-done.50, f32[8,64,128]{1,0,2:T(8,128)S(1)} %fusion.75, f32[8,64,127]{1,0,2:T(8,128)} %slice.461, f32[8,64,128]{1,0,2:T(8,128)S(1)} %get-tuple-element.20, f32[1,8,64,128]{2,1,3,0:T(8,128)} %copy-done.37), kind=kLoop, calls=%fused_computation.168 | loop fusion | flops 327680 | bytes 1832960 | tf_op jit(solution)/shard_map/add | solution.py:60
  43.7 2.0 %fusion.13 = (f32[2,8,64,128]{2,1,3,0:T(8,128)S(1)}, f32[2,8,64,128]{2,1,3,0:T(8,128)S(1)}) fusion(f32[1,8,64,128]{2,1,3,0:T(8,128)S(1)} %copy-done.35, f32[1,8,64,128]{2,1,3,0:T(8,128)S(1)} %bitcast.225, f32[2,1,64,128]{2,1,3,0:T(1,128)S(1)} %collective-permute-done.5, f32[1,8,64,128]{2,1,3,0:T(8,128)S(1)} %bitcast.228, f32[2,8,1,128]{2,1,3,0:T(8,128)} %copy.149), kind=kLoop, calls=%fused_computation.50 | loop fusion | flops 1048576 | bytes 1908736 | tf_op jit(solution)/shard_map/sub | solution.py:47
  51.2 3.9 %collective-permute-done.7 = f32[2,1,64,128]{2,1,3,0:T(1,128)S(1)} collective-permute-done((f32[2,1,64,128]{2,1,3,0:T(1,128)S(1)}, f32[2,1,64,128]{2,1,3,0:T(1,128)S(1)}, u32[]{:S(2)}, u32[]{:S(2)}) %collective-permute-start.7) | collective-permute-done | bytes 65568 | tf_op jit(solution)/shard_map/ppermute | solution.py:18
  55.1 1.7 %fusion.11 = (f32[2,8,64,128]{2,1,3,0:T(8,128)S(1)}, f32[2,8,64,128]{2,1,3,0:T(8,128)S(1)}) fusion(f32[1,8,64,128]{2,1,3,0:T(8,128)S(1)} %copy-done.28, f32[1,8,64,128]{2,1,3,0:T(8,128)S(1)} %bitcast.235, f32[2,1,64,128]{2,1,3,0:T(1,128)S(1)} %collective-permute-done.7, f32[1,8,64,128]{2,1,3,0:T(8,128)S(1)} %bitcast.237, f32[2,8,1,128]{2,1,3,0:T(8,128)} %copy.152), kind=kLoop, calls=%fused_computation.48 | loop fusion | flops 1048576 | bytes 1908736 | tf_op jit(solution)/shard_map/sub | solution.py:57
  64.9 2.0 %fusion.9 = (f32[2,8,64,128]{2,1,3,0:T(8,128)S(1)}, f32[2,8,64,128]{2,1,3,0:T(8,128)S(1)}) fusion(f32[1,8,64,128]{2,1,3,0:T(8,128)S(1)} %copy-done.31, f32[1,8,64,128]{2,1,3,0:T(8,128)S(1)} %bitcast.213, f32[2,1,64,128]{2,1,3,0:T(1,128)S(1)} %collective-permute-done.9, f32[1,8,64,128]{2,1,3,0:T(8,128)S(1)} %bitcast.216, f32[2,8,1,128]{2,1,3,0:T(8,128)} %copy.155), kind=kLoop, calls=%fused_computation.46 | loop fusion | flops 1048576 | bytes 1908736 | tf_op jit(solution)/shard_map/sub | solution.py:47
  70.8 1.4 copy.157
  77.9 2.3 %fusion.7 = (f32[2,8,64,128]{2,1,3,0:T(8,128)S(1)}, f32[2,8,64,128]{2,1,3,0:T(8,128)S(1)}) fusion(f32[1,8,64,128]{2,1,3,0:T(8,128)} %copy-done.25, f32[1,8,64,128]{2,1,3,0:T(8,128)S(1)} %bitcast.231, f32[2,1,64,128]{2,1,3,0:T(1,128)S(1)} %collective-permute-done.11, f32[1,8,64,128]{2,1,3,0:T(8,128)S(1)} %bitcast.233, f32[2,8,1,128]{2,1,3,0:T(8,128)} %copy.158), kind=kLoop, calls=%fused_computation.44 | loop fusion | flops 1048576 | bytes 1908736 | tf_op jit(solution)/shard_map/sub | solution.py:57
  83.0 3.4 %collective-permute-start.13 = (f32[2,1,64,128]{2,1,3,0:T(1,128)S(1)}, f32[2,1,64,128]{2,1,3,0:T(1,128)S(1)}, u32[]{:S(2)}, u32[]{:S(2)}) collective-permute-start(f32[2,1,64,128]{2,1,3,0:T(1,128)S(1)} %fusion.90), channel_id=1, source_target_pairs={{0,14},{2,0},{4,2},{6,4},{8,6},{10,8},{12,10},{14,12},{1,15},{3,1}... | collective-permute-start | bytes 196616 | tf_op jit(solution)/shard_map/ppermute | solution.py:18
  92.3 2.5 %fusion.5 = (f32[2,8,64,128]{2,1,3,0:T(8,128)S(1)}, f32[2,8,64,128]{2,1,3,0:T(8,128)S(1)}) fusion(f32[1,8,64,128]{2,1,3,0:T(8,128)} %copy-done.21, f32[1,8,64,128]{2,1,3,0:T(8,128)S(1)} %bitcast.219, f32[2,1,64,128]{2,1,3,0:T(1,128)S(1)} %collective-permute-done.13, f32[1,8,64,128]{2,1,3,0:T(8,128)S(1)} %bitcast.222, f32[2,8,1,128]{2,1,3,0:T(8,128)} %copy.161), kind=kLoop, calls=%fused_computation.42 | loop fusion | flops 1048576 | bytes 1908736 | tf_op jit(solution)/shard_map/sub | solution.py:47
  99.9 2.1 %slice.516 = f32[1,8,1,128]{2,1,3,0:T(8,128)} slice(f32[1,8,64,128]{2,1,3,0:T(8,128)} %bitcast.245), slice={[0:1], [0:8], [63:64], [0:128]} | slice | bytes 8192 | tf_op jit(solution)/shard_map/slice | solution.py:55
  103.7 2.6 %pad_maximum_fusion.1 = f32[3,8,64,128]{2,1,3,0:T(8,128)} fusion(f32[1,8,64,128]{2,1,3,0:T(8,128)} %copy-done.33, f32[1,8,64,128]{2,1,3,0:T(8,128)} %bitcast.243, f32[1,8,64,128]{2,1,3,0:T(8,128)} %bitcast.246), kind=kLoop, calls=%fused_computation.1 | loop fusion | flops 393216 | bytes 1572864 | tf_op jit(solution)/shard_map/stack | solution.py:53
  108.0 2.7 %copy.170 = f32[3,8,64,128]{3,2,1,0:T(8,128)} copy(f32[3,8,64,128]{2,1,3,0:T(8,128)} %pad_maximum_fusion.1) | data formatting | bytes 1572864
  112.1 3.0 %fusion.3 = (f32[2,8,64,128]{2,1,3,0:T(8,128)S(1)}, f32[2,8,64,128]{2,1,3,0:T(8,128)S(1)}) fusion(f32[1,8,64,128]{2,1,3,0:T(8,128)} %copy-done.33, f32[1,8,64,128]{2,1,3,0:T(8,128)} %bitcast.244, f32[2,1,64,128]{2,1,3,0:T(1,128)S(1)} %collective-permute-done.15, f32[1,8,64,128]{2,1,3,0:T(8,128)} %bitcast.247, f32[2,8,1,128]{2,1,3,0:T(8,128)} %copy.164), kind=kLoop, calls=%fused_computation.40 | loop fusion | flops 1048576 | bytes 1908736 | tf_op jit(solution)/shard_map/sub | solution.py:57
  117.4 1.4 copy.169
  121.5 1.4 fusion.1
  122.8 1.4 fusion
  124.3 21.4 %all-reduce.16 = f32[64,4]{0,1:T(4,128)S(1)} all-reduce(f32[64,4]{0,1:T(4,128)S(1)} %pad_maximum_fusion.59), channel_id=2, replica_groups=mesh['clip'=2,'gx'=8,'gy'=2] {'gx'}, use_global_device_ids=true, to_apply=%region_2.3.clone | all-reduce | flops 256 | bytes 2048
  145.8 2.4 %psum.7 = f32[8,4]{0,1:T(4,128)S(1)} all-reduce(f32[8,4]{0,1:T(4,128)S(1)} %constant_dynamic-slice_fusion), channel_id=1, replica_groups=mesh['clip'=2,'gx'=8,'gy'=2] {'gy'}, use_global_device_ids=true, to_apply=%region_3.4 | all-reduce | flops 32 | bytes 256 | tf_op jit(solution)/shard_map/psum | solution.py:113
  (284 shorter events, 71.9 us)
Async XLA Ops:
  0.6 9.1 %copy-start.67 = (f32[3,8,64,128]{3,2,1,0:T(8,128)S(1)}, f32[3,8,64,128]{3,2,1,0:T(8,128)}, u32[]{:S(2)}) copy-start(f32[3,8,64,128]{3,2,1,0:T(8,128)} %param.7) | copy-start | bytes 2359300
  1.5 14.4 %collective-permute-start = (f32[2,8,1,128]{3,1,2,0:T(8,128)S(1)}, f32[2,8,1,128]{3,1,2,0:T(8,128)S(1)}, u32[]{:S(2)}, u32[]{:S(2)}) collective-permute-start(f32[2,8,1,128]{3,1,2,0:T(8,128)S(1)} %pad_maximum_fusion.51), channel_id=1, source_target_pairs={{0,1},{1,0},{2,3},{3,2},{4,5},{5,4},{6,7},{7,6},{8,9},{9,8},{10,11... | collective-permute-start | bytes 24584 | tf_op jit(solution)/shard_map/ppermute | solution.py:18
  3.0 16.0 %collective-permute-start.1 = (f32[2,1,64,128]{2,1,3,0:T(1,128)S(1)}, f32[2,1,64,128]{2,1,3,0:T(1,128)S(1)}, u32[]{:S(2)}, u32[]{:S(2)}) collective-permute-start(f32[2,1,64,128]{2,1,3,0:T(1,128)S(1)} %copy.141), channel_id=1, source_target_pairs={{0,14},{2,0},{4,2},{6,4},{8,6},{10,8},{12,10},{14,12},{1,15},{3,1}... | collective-permute-start | bytes 196616 | tf_op jit(solution)/shard_map/ppermute | solution.py:18
  11.3 10.7 %copy-start.37 = (f32[1,8,64,128]{2,1,3,0:T(8,128)}, f32[1,8,64,128]{2,1,3,0:T(8,128)S(1)}, u32[]{:S(2)}) copy-start(f32[1,8,64,128]{2,1,3,0:T(8,128)S(1)} %copy.173) | copy-start | bytes 786436
  21.1 10.5 %copy-start.23 = (f32[1,8,64,128]{2,1,3,0:T(8,128)}, f32[1,8,64,128]{2,1,3,0:T(8,128)S(1)}, u32[]{:S(2)}) copy-start(f32[1,8,64,128]{2,1,3,0:T(8,128)S(1)} %fusion.80) | copy-start | bytes 786436
  23.0 8.5 %collective-permute-start.3 = (f32[2,1,64,128]{2,1,3,0:T(1,128)}, f32[2,1,64,128]{2,1,3,0:T(1,128)S(1)}, u32[]{:S(2)}, u32[]{:S(2)}) collective-permute-start(f32[2,1,64,128]{2,1,3,0:T(1,128)} %fusion.95), channel_id=1, source_target_pairs={{0,2},{2,4},{4,6},{6,8},{8,10},{10,12},{12,14},{14,0},{1,3},{3,5},... | collective-permute-start | bytes 196616 | tf_op jit(solution)/shard_map/ppermute | solution.py:18
  24.2 3.5 %collective-permute-start.2 = (f32[2,8,1,128]{3,1,2,0:T(8,128)S(1)}, f32[2,8,1,128]{3,1,2,0:T(8,128)S(1)}, u32[]{:S(2)}, u32[]{:S(2)}) collective-permute-start(f32[2,8,1,128]{3,1,2,0:T(8,128)S(1)} %pad_maximum_fusion.52), channel_id=1, source_target_pairs={{0,1},{1,0},{2,3},{3,2},{4,5},{5,4},{6,7},{7,6},{8,9},{9,8},{10,11... | collective-permute-start | bytes 24584 | tf_op jit(solution)/shard_map/ppermute | solution.py:18
  25.0 8.2 %copy-start.46 = (f32[8,64,128]{1,0,2:T(8,128)}, f32[8,64,128]{1,0,2:T(8,128)S(1)}, u32[]{:S(2)}) copy-start(f32[8,64,128]{1,0,2:T(8,128)S(1)} %copy.130) | copy-start | bytes 786436
  36.9 6.8 %collective-permute-start.5 = (f32[2,1,64,128]{2,1,3,0:T(1,128)S(1)}, f32[2,1,64,128]{2,1,3,0:T(1,128)S(1)}, u32[]{:S(2)}, u32[]{:S(2)}) collective-permute-start(f32[2,1,64,128]{2,1,3,0:T(1,128)S(1)} %fusion.94), channel_id=1, source_target_pairs={{0,14},{2,0},{4,2},{6,4},{8,6},{10,8},{12,10},{14,12},{1,15},{3,1}... | collective-permute-start | bytes 196616 | tf_op jit(solution)/shard_map/ppermute | solution.py:18
  41.1 1.2 collective-permute-start.4
  46.7 8.4 %collective-permute-start.7 = (f32[2,1,64,128]{2,1,3,0:T(1,128)S(1)}, f32[2,1,64,128]{2,1,3,0:T(1,128)S(1)}, u32[]{:S(2)}, u32[]{:S(2)}) collective-permute-start(f32[2,1,64,128]{2,1,3,0:T(1,128)S(1)} %fusion.93), channel_id=1, source_target_pairs={{0,2},{2,4},{4,6},{6,8},{8,10},{10,12},{12,14},{14,0},{1,3},{3,5},... | collective-permute-start | bytes 196616 | tf_op jit(solution)/shard_map/ppermute | solution.py:18
  47.2 9.9 %copy-start.6 = (f32[8,64,128]{1,0,2:T(8,128)}, f32[8,64,128]{1,0,2:T(8,128)S(1)}, u32[]{:S(2)}) copy-start(f32[8,64,128]{1,0,2:T(8,128)S(1)} %fusion.70) | copy-start | bytes 786436
  47.8 7.3 %copy-start.28 = (f32[1,8,64,128]{2,1,3,0:T(8,128)S(1)}, f32[1,8,64,128]{2,1,3,0:T(8,128)}, u32[]{:S(2)}) copy-start(f32[1,8,64,128]{2,1,3,0:T(8,128)} %copy-done.27) | copy-start | bytes 786436
  47.8 2.0 %collective-permute-start.6 = (f32[2,8,1,128]{3,1,2,0:T(8,128)S(1)}, f32[2,8,1,128]{3,1,2,0:T(8,128)S(1)}, u32[]{:S(2)}, u32[]{:S(2)}) collective-permute-start(f32[2,8,1,128]{3,1,2,0:T(8,128)S(1)} %pad_maximum_fusion.54), channel_id=1, source_target_pairs={{0,1},{1,0},{2,3},{3,2},{4,5},{5,4},{6,7},{7,6},{8,9},{9,8},{10,11... | collective-permute-start | bytes 24584 | tf_op jit(solution)/shard_map/ppermute | solution.py:18
  59.3 5.6 %collective-permute-start.9 = (f32[2,1,64,128]{2,1,3,0:T(1,128)S(1)}, f32[2,1,64,128]{2,1,3,0:T(1,128)S(1)}, u32[]{:S(2)}, u32[]{:S(2)}) collective-permute-start(f32[2,1,64,128]{2,1,3,0:T(1,128)S(1)} %fusion.92), channel_id=1, source_target_pairs={{0,14},{2,0},{4,2},{6,4},{8,6},{10,8},{12,10},{14,12},{1,15},{3,1}... | collective-permute-start | bytes 196616 | tf_op jit(solution)/shard_map/ppermute | solution.py:18
  61.8 1.8 %collective-permute-start.8 = (f32[2,8,1,128]{3,1,2,0:T(8,128)S(1)}, f32[2,8,1,128]{3,1,2,0:T(8,128)S(1)}, u32[]{:S(2)}, u32[]{:S(2)}) collective-permute-start(f32[2,8,1,128]{3,1,2,0:T(8,128)S(1)} %pad_maximum_fusion.55), channel_id=1, source_target_pairs={{0,1},{1,0},{2,3},{3,2},{4,5},{5,4},{6,7},{7,6},{8,9},{9,8},{10,11... | collective-permute-start | bytes 24584 | tf_op jit(solution)/shard_map/ppermute | solution.py:18
  68.1 9.8 %copy-start = (f32[8,64,128]{1,0,2:T(8,128)}, f32[8,64,128]{1,0,2:T(8,128)S(1)}, u32[]{:S(2)}) copy-start(f32[8,64,128]{1,0,2:T(8,128)S(1)} %fusion.43) | copy-start | bytes 786436
  69.3 8.6 %collective-permute-start.11 = (f32[2,1,64,128]{2,1,3,0:T(1,128)S(1)}, f32[2,1,64,128]{2,1,3,0:T(1,128)S(1)}, u32[]{:S(2)}, u32[]{:S(2)}) collective-permute-start(f32[2,1,64,128]{2,1,3,0:T(1,128)S(1)} %fusion.91), channel_id=1, source_target_pairs={{0,2},{2,4},{4,6},{6,8},{8,10},{10,12},{12,14},{14,0},{1,3},{3,5},... | collective-permute-start | bytes 196616 | tf_op jit(solution)/shard_map/ppermute | solution.py:18
  70.8 7.2 %copy-start.3 = (f32[8,64,128]{1,0,2:T(8,128)}, f32[8,64,128]{1,0,2:T(8,128)S(1)}, u32[]{:S(2)}) copy-start(f32[8,64,128]{1,0,2:T(8,128)S(1)} %fusion.54) | copy-start | bytes 786436
  74.4 2.0 %collective-permute-start.10 = (f32[2,8,1,128]{3,1,2,0:T(8,128)S(1)}, f32[2,8,1,128]{3,1,2,0:T(8,128)S(1)}, u32[]{:S(2)}, u32[]{:S(2)}) collective-permute-start(f32[2,8,1,128]{3,1,2,0:T(8,128)S(1)} %pad_maximum_fusion.56), channel_id=1, source_target_pairs={{0,1},{1,0},{2,3},{3,2},{4,5},{5,4},{6,7},{7,6},{8,9},{9,8},{10,11... | collective-permute-start | bytes 24584 | tf_op jit(solution)/shard_map/ppermute | solution.py:18
  83.0 9.2 %collective-permute-start.13 = (f32[2,1,64,128]{2,1,3,0:T(1,128)S(1)}, f32[2,1,64,128]{2,1,3,0:T(1,128)S(1)}, u32[]{:S(2)}, u32[]{:S(2)}) collective-permute-start(f32[2,1,64,128]{2,1,3,0:T(1,128)S(1)} %fusion.90), channel_id=1, source_target_pairs={{0,14},{2,0},{4,2},{6,4},{8,6},{10,8},{12,10},{14,12},{1,15},{3,1}... | collective-permute-start | bytes 196616 | tf_op jit(solution)/shard_map/ppermute | solution.py:18
  87.9 3.0 %collective-permute-start.12 = (f32[2,8,1,128]{3,1,2,0:T(8,128)S(1)}, f32[2,8,1,128]{3,1,2,0:T(8,128)S(1)}, u32[]{:S(2)}, u32[]{:S(2)}) collective-permute-start(f32[2,8,1,128]{3,1,2,0:T(8,128)S(1)} %pad_maximum_fusion.57), channel_id=1, source_target_pairs={{0,1},{1,0},{2,3},{3,2},{4,5},{5,4},{6,7},{7,6},{8,9},{9,8},{10,11... | collective-permute-start | bytes 24584 | tf_op jit(solution)/shard_map/ppermute | solution.py:18
  97.2 14.9 %collective-permute-start.15 = (f32[2,1,64,128]{2,1,3,0:T(1,128)S(1)}, f32[2,1,64,128]{2,1,3,0:T(1,128)S(1)}, u32[]{:S(2)}, u32[]{:S(2)}) collective-permute-start(f32[2,1,64,128]{2,1,3,0:T(1,128)S(1)} %fusion.89), channel_id=1, source_target_pairs={{0,2},{2,4},{4,6},{6,8},{8,10},{10,12},{12,14},{14,0},{1,3},{3,5},... | collective-permute-start | bytes 196616 | tf_op jit(solution)/shard_map/ppermute | solution.py:18
  103.2 7.6 %collective-permute-start.14 = (f32[2,8,1,128]{3,1,2,0:T(8,128)S(1)}, f32[2,8,1,128]{3,1,2,0:T(8,128)S(1)}, u32[]{:S(2)}, u32[]{:S(2)}) collective-permute-start(f32[2,8,1,128]{3,1,2,0:T(8,128)S(1)} %pad_maximum_fusion.58), channel_id=1, source_target_pairs={{0,1},{1,0},{2,3},{3,2},{4,5},{5,4},{6,7},{7,6},{8,9},{9,8},{10,11... | collective-permute-start | bytes 24584 | tf_op jit(solution)/shard_map/ppermute | solution.py:18
  (66 other events, 140.6 us)
where the time goes:
time: 150 us; the launch traced here: 149 us
  local copies, waits for them, and re-layouts  63.3 us (42%)
  other arithmetic  31.2 us (21%)
  blocking collectives  23.9 us (16%)
  starting transfers between devices  16.2 us (11%)
  waiting for transfers between devices  6.64 us (4%)
  matrix products  5.32 us (4%)
  between operations  2.26 us (2%)
    unnamed x1, blocking collectives  21.4 us
    unnamed x157, local copies, waits for them, and re-layouts  19.7 us
    ppermute x16, starting transfers between devices, shifted(): return lax.ppermute(value, axis, pairs)  16.2 us
    slice x16, local copies, waits for them, and re-layouts, split_step(): behind_y = shifted(jnp.stack([magn[0, :, -1:], magn[2, :, -1:]]), 'gy', 1)  13.6 us
    ppermute x8, local copies, waits for them, and re-layouts, shifted(): return lax.ppermute(value, axis, pairs)  9.8 us
    sub x4, other arithmetic, split_step(): bdiff_x = back_x[:, 1:] - back_x[:, :-1]  8.72 us
    sub x4, other arithmetic, split_step(): diff_x = ext_x[:, 1:] - ext_x[:, :-1]  8.38 us
    slice x8, local copies, waits for them, and re-layouts, backward_z(): field[..., :-1]  6.71 us
  transfers between devices with their start and end apart: 16, of which 4 were waited for; matrix products, arithmetic and copies ran while one was open for 36% of the time, Pallas kernels for 0%

commit v1 on v0

v1 whole, which is shorter than its diff:
```python
import functools
import math

import jax
import jax.numpy as jnp
from jax import lax
from jax.experimental import pallas as pl
from jax.experimental.pallas import tpu as pltpu
from jax.sharding import PartitionSpec as P

ITERS = 4
TIME_STEP = 0.5
PHASE_STEP = 0.9
MESH = pl.DeviceIdType.MESH
PAD = 8
HIGH = lax.Precision.HIGHEST

FWD, BACK, ROW_E, ROW_H, CORNER_E, CORNER_H = range(6)


def kernel(
    size_x, size_y,
    eps_ref, sigma_ref, orders_ref, e_in, h_in, mat_in,
    e_out, h_out, far_ref,
    elec, magn, mat, coef, mon, tables,
    fwd_send, fwd_recv, back_send, back_recv,
    rowe_send, rowe_recv, rowh_send, rowh_recv,
    core_send, core_recv, corh_send, corh_recv,
    terms_send, terms_recv,
    load_sem, store_sem, send_sem, recv_sem, far_send_sem, far_recv_sem,
):
    cells_x, cells_y, depth = mat.shape
    last = cells_x - 1
    chunk = min(32, cells_y)
    starts = range(0, cells_y, chunk)
    me_x = lax.axis_index("gx")
    me_y = lax.axis_index("gy")
    right = lax.rem(me_x + 1, size_x)
    left = lax.rem(me_x + size_x - 1, size_x)
    above = lax.rem(me_y + 1, size_y)
    below = lax.rem(me_y + size_y - 1, size_y)
    group = size_x * size_y
    me = me_x * size_y + me_y

    def load(src, dst, sem):
        copy = pltpu.make_async_copy(src, dst, load_sem.at[sem])
        copy.start()
        return copy

    inner = pl.ds(0, last)
    ebody = pl.ds(0, cells_y)
    hbody = pl.ds(PAD, cells_y)
    edge_e = load(e_in.at[:, last], elec.at[:, last, ebody], 0)
    edge_h = load(h_in.at[:, last], magn.at[:, last, hbody], 1)
    rest_e = load(e_in.at[:, inner], elec.at[:, inner, ebody], 2)
    rest_h = load(h_in.at[:, inner], magn.at[:, inner, hbody], 3)
    load_mat = load(mat_in, mat, 4)

    def member(offset):
        index = lax.rem(me + offset, group)
        return index // size_y, lax.rem(index, size_y)

    barrier = pltpu.get_barrier_semaphore()
    for offset in range(1, group):
        tx, ty = member(offset)
        pl.semaphore_signal(barrier, inc=1, device_id={"gx": tx, "gy": ty}, device_id_type=MESH)

    lane = lax.broadcasted_iota(jnp.int32, (chunk, depth), 1)
    first_lane = lane == 0
    last_lane = lane == depth - 1

    def forward_z(value):
        return jnp.where(last_lane, 0.0, pltpu.roll(value, depth - 1, 1)) - value

    def backward_z(value):
        return value - jnp.where(first_lane, 0.0, pltpu.roll(value, 1, 1))

    elec[:, :, pl.ds(cells_y, PAD), :] = jnp.zeros((3, cells_x, PAD, depth), jnp.float32)

    def copy_to(phase, kind, src, dst, tx, ty):
        return pltpu.make_async_remote_copy(
            src_ref=src, dst_ref=dst,
            send_sem=send_sem.at[phase, kind], recv_sem=recv_sem.at[phase, kind],
            device_id={"gx": tx, "gy": ty}, device_id_type=MESH,
        )

    def fwd_copy(k):
        return copy_to(k, FWD, fwd_send.at[k], fwd_recv.at[k], right, me_y)

    def back_copy(k):
        src = e_in.at[pl.ds(1, 2), 0] if k == 0 else back_send.at[k]
        return copy_to(k, BACK, src, back_recv.at[k], left, me_y)

    def rowe_copy(k):
        return copy_to(k, ROW_E, rowe_send.at[k], rowe_recv.at[k], me_x, below)

    def rowh_copy(k):
        return copy_to(k, ROW_H, rowh_send.at[k], rowh_recv.at[k], me_x, above)

    def core_copy(k):
        return copy_to(k, CORNER_E, core_send.at[k], core_recv.at[k], right, below)

    def corh_copy(k):
        return copy_to(k, CORNER_H, corh_send.at[k], corh_recv.at[k], left, above)

    def magn_plane(x, ahead, stage=None):
        for r in starts:
            rows, upper, hrows = pl.ds(r, chunk), pl.ds(r + 1, chunk), pl.ds(PAD + r, chunk)
            ex, ey, ez = elec[0, x, rows], elec[1, x, rows], elec[2, x, rows]
            dyx = elec[0, x, upper] - ex
            dyz = elec[2, x, upper] - ez
            if ahead is None:
                dxy, dxz = -ey, -ez
            else:
                dxy, dxz = elec[1, ahead, rows] - ey, elec[2, ahead, rows] - ez
            hy = magn[1, x, hrows] - TIME_STEP * (forward_z(ex) - dxz)
            hz = magn[2, x, hrows] - TIME_STEP * (dxy - dyx)
            magn[0, x, hrows] = magn[0, x, hrows] - TIME_STEP * (dyz - forward_z(ey))
            magn[1, x, hrows] = hy
            magn[2, x, hrows] = hz
            if stage is not None:
                fwd_send[stage, 0, rows] = hy
                fwd_send[stage, 1, rows] = hz

    def elec_plane(x, previous, number, stage=None):
        cos_n = math.cos(PHASE_STEP * number)
        sin_n = math.sin(PHASE_STEP * number)
        for r in starts:
            rows, hrows, lower = pl.ds(r, chunk), pl.ds(PAD + r, chunk), pl.ds(PAD + r - 1, chunk)
            hx, hy, hz = magn[0, x, hrows], magn[1, x, hrows], magn[2, x, hrows]
            ex, ey, ez = elec[0, x, rows], elec[1, x, rows], elec[2, x, rows]
            prev_y, prev_z = previous(r, ey, ez)
            keep, drive = coef[0, x, rows], coef[1, x, rows]
            new_x = keep * ex + drive * ((hz - magn[2, x, lower]) - backward_z(hy))
            new_y = keep * ey + drive * (backward_z(hx) - (hz - prev_z))
            new_z = keep * ez + drive * ((hy - prev_y) - (hx - magn[0, x, lower]))
            elec[0, x, rows] = new_x
            elec[1, x, rows] = new_y
            elec[2, x, rows] = new_z
            if stage is not None:
                back_send[stage, 0, rows] = new_y
                back_send[stage, 1, rows] = new_z
            total = mon[rows]
            for comp, new in ((0, new_x), (1, new_y)):
                slot = comp * cells_x + x
                weight = jnp.where(lane == slot, cos_n, jnp.where(lane == slot + 2 * cells_x, -sin_n, 0.0))
                total = total + jnp.broadcast_to(new[:, depth - 3:depth - 2], (chunk, depth)) * weight
            mon[rows] = total

    def local_previous(x):
        def previous(r, ey, ez):
            hrows = pl.ds(PAD + r, chunk)
            return magn[1, x - 1, hrows], magn[2, x - 1, hrows]
        return previous

    def send_back(k):
        if k == 0:
            corh_send[k] = elec[1, 0, pl.ds(cells_y - 8, 8)]
        else:
            corh_send[k] = back_send[k, 0, pl.ds(cells_y - 8, 8)]
            back_copy(k).start()
        corh_copy(k).start()

    def send_fwd(k):
        core_send[k] = elec[0, last, pl.ds(0, 8)]
        fwd_copy(k).start()
        core_copy(k).start()

    mon[...] = jnp.zeros_like(mon)
    edge_e.wait()
    edge_h.wait()
    magn_plane(last, None, 0)
    pl.semaphore_wait(barrier, group - 1)
    back_copy(0).start()
    send_fwd(0)
    rest_e.wait()
    send_back(0)
    rest_h.wait()

    row63 = pl.ds(PAD + cells_y - 1, 1)
    halo = pl.ds(PAD - 1, 1)
    row0 = pl.ds(0, 1)

    stores = []

    def store(src, dst):
        copy = pltpu.make_async_copy(src, dst, store_sem.at[len(stores)])
        copy.start()
        stores.append(copy)

    for k in range(ITERS):
        def magn_body(x, carry):
            magn_plane(x, x + 1)
            return carry

        lax.fori_loop(0, last, magn_body, 0)
        rowe_send[k, 0] = elec[0, :, row0]
        rowe_send[k, 1] = elec[2, :, row0]
        rowh_send[k, 0] = magn[0, :, row63]
        rowh_send[k, 1] = magn[2, :, row63]
        rowe_copy(k).start()
        rowh_copy(k).start()
        if k == 0:
            load_mat.wait()
            count = eps_ref.shape[0]
            keeps, drives = [], []
            for m in range(count):
                permit = jnp.full((8, depth), eps_ref[m], jnp.float32)
                conduct = jnp.full((8, depth), sigma_ref[m], jnp.float32)
                loss = conduct * TIME_STEP / (2.0 * permit)
                keeps.append(((1.0 - loss) / (1.0 + loss))[:1])
                drives.append((TIME_STEP / (permit * (1.0 + loss)))[:1])

            def coef_body(x, carry):
                for r in starts:
                    rows = pl.ds(r, chunk)
                    ids = mat[x, rows]
                    keep = jnp.broadcast_to(keeps[0], (chunk, depth))
                    drive = jnp.broadcast_to(drives[0], (chunk, depth))
                    for m in range(1, count):
                        keep = jnp.where(ids == m, keeps[m], keep)
                        drive = jnp.where(ids == m, drives[m], drive)
                    coef[0, x, rows] = keep
                    coef[1, x, rows] = drive
                return carry

            lax.fori_loop(0, cells_x, coef_body, 0)
        if k == 1:
            shape = (orders_ref.shape[0], depth)
            wide = lax.broadcasted_iota(jnp.int32, shape, 1)
            for slot, axis, pos, extent in (
                (0, 1, me_y * cells_y + wide, size_y * cells_y),
                (2, 0, me_x * cells_x + lax.rem(wide, cells_x), size_x * cells_x),
            ):
                order = jnp.broadcast_to(orders_ref[:, axis:axis + 1], shape)
                turns = (order * pos).astype(jnp.float32) * (1.0 / extent)
                angle = (turns - jnp.floor(turns)) * (2.0 * math.pi)
                tables[slot] = jnp.cos(angle)
                tables[slot + 1] = jnp.sin(angle)

        rowe_copy(k).wait_recv()
        rowh_copy(k).wait_recv()
        magn[0, :, row63] = magn[0, :, row63] - TIME_STEP * rowe_recv[k, 1]
        magn[2, :, row63] = magn[2, :, row63] + TIME_STEP * rowe_recv[k, 0]
        magn[0, :, halo] = rowh_recv[k, 0] - TIME_STEP * elec[2, :, row0]
        magn[2, :, halo] = rowh_recv[k, 1] + TIME_STEP * elec[0, :, row0]

        def elec_body(x, carry):
            elec_plane(x, local_previous(x), k + 1)
            return carry

        lax.fori_loop(1, last, elec_body, 0)
        final = k == ITERS - 1
        if final:
            store(magn.at[:, inner, hbody], h_out.at[:, inner])
            store(elec.at[:, pl.ds(1, last - 1), ebody], e_out.at[:, pl.ds(1, last - 1)])

        fwd_copy(k).wait_recv()
        core_copy(k).wait_recv()
        fwd_recv[k, 1, pl.ds(cells_y - 1, 1)] = (
            fwd_recv[k, 1, pl.ds(cells_y - 1, 1)] + TIME_STEP * core_recv[k, pl.ds(0, 1)]
        )

        def received(r, ey, ez):
            rows = pl.ds(r, chunk)
            return fwd_recv[k, 0, rows] + TIME_STEP * ez, fwd_recv[k, 1, rows] - TIME_STEP * ey

        elec_plane(0, received, k + 1, None if final else k + 1)
        if not final:
            send_back(k + 1)
        else:
            store(elec.at[:, 0, ebody], e_out.at[:, 0])

        back_copy(k).wait_recv()
        corh_copy(k).wait_recv()
        for r in starts:
            rows, hrows = pl.ds(r, chunk), pl.ds(PAD + r, chunk)
            magn[1, last, hrows] = magn[1, last, hrows] + TIME_STEP * back_recv[k, 1, rows]
            magn[2, last, hrows] = magn[2, last, hrows] - TIME_STEP * back_recv[k, 0, rows]
        magn[2, last, halo] = magn[2, last, halo] - TIME_STEP * corh_recv[k, pl.ds(7, 1)]
        elec_plane(last, local_previous(last), k + 1)
        if not final:
            magn_plane(last, None, k + 1)
            send_fwd(k + 1)
        else:
            store(magn.at[:, last, hbody], h_out.at[:, last])
            store(elec.at[:, last, ebody], e_out.at[:, last])

    span = 2 * cells_x
    total = mon[...]
    by_cos = jnp.dot(tables[0, :, pl.ds(0, cells_y)], total, precision=HIGH, preferred_element_type=jnp.float32)
    by_sin = jnp.dot(tables[1, :, pl.ds(0, cells_y)], total, precision=HIGH, preferred_element_type=jnp.float32)
    part_re = by_cos + pltpu.roll(by_sin, depth - span, 1)
    part_im = pltpu.roll(by_cos, depth - span, 1) - by_sin
    cos_x, sin_x = tables[2], tables[3]
    wide = lax.broadcasted_iota(jnp.int32, part_re.shape, 1)
    real = jnp.where(wide < span, cos_x * part_re + sin_x * part_im, 0.0)
    imag = jnp.where(wide < span, cos_x * part_im - sin_x * part_re, 0.0)
    both = real + pltpu.roll(imag, span, 1)
    owned = terms_send.shape[1]
    for peer in range(size_x):
        terms_send[peer] = both[peer * owned:(peer + 1) * owned]

    def far_copy(offset):
        tx, ty = member(offset)
        return pltpu.make_async_remote_copy(
            src_ref=terms_send.at[tx], dst_ref=terms_recv.at[me],
            send_sem=far_send_sem.at[offset], recv_sem=far_recv_sem.at[me],
            device_id={"gx": tx, "gy": ty}, device_id_type=MESH,
        )

    for offset in range(1, group):
        far_copy(offset).start()
    answer = terms_send[me_x]
    for offset in range(1, group):
        source = lax.rem(me + offset, group)
        pltpu.make_async_remote_copy(
            src_ref=terms_send.at[0], dst_ref=terms_recv.at[source],
            send_sem=far_send_sem.at[offset], recv_sem=far_recv_sem.at[source],
            device_id={"gx": right, "gy": me_y}, device_id_type=MESH,
        ).wait_recv()
        answer = answer + terms_recv[source]
    source_lane = lax.broadcasted_iota(jnp.int32, (depth, depth), 0) // cells_x
    target_lane = lax.broadcasted_iota(jnp.int32, (depth, depth), 1)
    picked = jnp.where(source_lane < 2, 2 * source_lane, 2 * source_lane - 3)
    pick = jnp.where((source_lane < 4) & (picked == target_lane), 1.0, 0.0)
    summed = jnp.dot(answer, pick, precision=HIGH, preferred_element_type=jnp.float32)
    scale = 1.0 / math.sqrt(size_x * cells_x * size_y * cells_y)
    far_ref[...] = summed[:, :4] * scale

    for copy in stores:
        copy.wait()
    for k in range(ITERS):
        for copy in (fwd_copy, back_copy, rowe_copy, rowh_copy, core_copy, corh_copy):
            copy(k).wait_send()
    for offset in range(1, group):
        far_copy(offset).wait_send()


def local(size_x, size_y, e_field, h_field, material, eps_table, sigma_table, angle_orders):
    cells_x, cells_y, depth = material.shape
    angles = angle_orders.shape[0]
    owned = angles // size_x
    group = size_x * size_y
    f32 = jnp.float32
    vmem = functools.partial(pl.BlockSpec, memory_space=pltpu.VMEM)
    smem = functools.partial(pl.BlockSpec, memory_space=pltpu.SMEM)
    hbm = functools.partial(pl.BlockSpec, memory_space=pl.ANY)
    dma = pltpu.SemaphoreType.DMA
    planes = pltpu.VMEM((ITERS, 2, cells_y, depth), f32)
    rows = pltpu.VMEM((ITERS, 2, cells_x, 1, depth), f32)
    corner = pltpu.VMEM((ITERS, 8, depth), f32)
    return pl.pallas_call(
        functools.partial(kernel, size_x, size_y),
        out_shape=(
            jax.ShapeDtypeStruct(e_field.shape, f32),
            jax.ShapeDtypeStruct(h_field.shape, f32),
            jax.ShapeDtypeStruct((owned, 4), f32),
        ),
        in_specs=[smem(), smem(), vmem(), hbm(), hbm(), hbm()],
        out_specs=(hbm(), hbm(), vmem()),
        scratch_shapes=[
            pltpu.VMEM((3, cells_x, cells_y + PAD, depth), f32),
            pltpu.VMEM((3, cells_x, cells_y + PAD, depth), f32),
            pltpu.VMEM((cells_x, cells_y, depth), jnp.int32),
            pltpu.VMEM((2, cells_x, cells_y, depth), f32),
            pltpu.VMEM((cells_y, depth), f32),
            pltpu.VMEM((4, angles, depth), f32),
            planes, planes, planes, planes,
            rows, rows, rows, rows,
            corner, corner, corner, corner,
            pltpu.VMEM((size_x, owned, depth), f32),
            pltpu.VMEM((group, owned, depth), f32),
            dma((5,)), dma((5,)), dma((ITERS, 6)), dma((ITERS, 6)), dma((group,)), dma((group,)),
        ],
        compiler_params=pltpu.CompilerParams(
            collective_id=0, has_side_effects=True, vmem_limit_bytes=32 * 1024 * 1024
        ),
    )(eps_table, sigma_table, angle_orders, e_field, h_field, material)


def solution(mesh):
    return jax.shard_map(
        functools.partial(local, mesh.shape["gx"], mesh.shape["gy"]),
        mesh=mesh,
        in_specs=(
            P(None, ("clip", "gx"), "gy", None),
            P(None, ("clip", "gx"), "gy", None),
            P(("clip", "gx"), "gy", None),
            P(),
            P(),
            P(),
        ),
        out_specs=(
            P(None, ("clip", "gx"), "gy", None),
            P(None, ("clip", "gx"), "gy", None),
            P(("clip", "gx"), None),
        ),
        check_vma=False,
    )
```

time: 150 us -> 38 us (0.25)
  local copies, waits for them, and re-layouts: 63.3 us -> 6.41 us
  other arithmetic: 31.2 us -> 0 us
  Pallas kernels: 0 us -> 30.7 us
  blocking collectives: 23.9 us -> 0 us
  starting transfers between devices: 16.2 us -> 0 us
  waiting for transfers between devices: 6.64 us -> 0 us
  matrix products: 5.32 us -> 0 us
  between operations: 2.26 us -> 0.67 us
    slice x47 -> x0, local copies, waits for them, and re-layouts: 32.6 us -> none  [the longest x16 13.6 us: split_step(): behind_y = shifted(jnp.stack([magn[0, :, -1:], magn[2, :, -1:]]), 'gy', 1)]
    pallas_call x0 -> x1, Pallas kernels: none -> 30.7 us  [local(): pl.pallas_call(functools.partial(kernel, size_x, size_y), out_shape=(jax....]
    unnamed x1 -> x0, blocking collectives: 21.4 us -> none
    sub x22 -> x0, other arithmetic: 20 us -> none  [the longest x4 8.72 us: split_step(): bdiff_x = back_x[:, 1:] - back_x[:, :-1]]
    ppermute x16 -> x0, starting transfers between devices: 16.2 us -> none  [shifted(): return lax.ppermute(value, axis, pairs)]
    unnamed x157 -> x13, local copies, waits for them, and re-layouts: 19.7 us -> 5.76 us
    ppermute x8 -> x0, local copies, waits for them, and re-layouts: 9.8 us -> none  [shifted(): return lax.ppermute(value, axis, pairs)]
    ppermute x16 -> x0, waiting for transfers between devices: 6.64 us -> none  [shifted(): return lax.ppermute(value, axis, pairs)]
  transfers between devices with their start and end apart: 16 -> 0, of which waited for: 4 -> 0; matrix products, arithmetic and copies ran while one was open for 36% -> 0% of each run, Pallas kernels for 0% -> 0%
where the time goes in v1:
time: 38 us; the launch traced here: 37.8 us
  Pallas kernels  30.7 us (81%)
  local copies, waits for them, and re-layouts  6.41 us (17%)
  between operations  0.67 us (2%)
    pallas_call x1, Pallas kernels, local(): pl.pallas_call(functools.partial(kernel, size_x, size_y), out_shape=(jax....  30.7 us
    unnamed x13, local copies, waits for them, and re-layouts  5.76 us

profile of v1, /device:TPU:0, one launch (start us, length us, event | category | flops | bytes accessed | tf_op | source)
XLA Modules:
  0.0 37.8 jit_solution(4082184405562688715)
XLA Ops:
  0.6 0.0 copy-start.4
  0.6 0.0 copy-start.3
  0.7 0.8 %copy.9.orders_ref = s32[64,2]{1,0:T(8,128)S(1)} copy(s32[64,2]{0,1:T(2,128)} %param.11) | data formatting | bytes 1024 | tf_op args[5]
  1.4 0.0 copy-done.4
  1.4 0.0 copy-done.3
  1.4 0.0 copy-start
  1.5 1.1 %copy-done = f32[3,8,64,128]{3,2,1,0:T(8,128)S(1)} copy-done((f32[3,8,64,128]{3,2,1,0:T(8,128)S(1)}, f32[3,8,64,128]{3,2,1,0:T(8,128)}, u32[]{:S(2)}) %copy-start) | copy-done | bytes 786456
  2.6 0.0 copy-start.1
  2.6 1.1 %copy-done.1 = f32[3,8,64,128]{3,2,1,0:T(8,128)S(1)} copy-done((f32[3,8,64,128]{3,2,1,0:T(8,128)S(1)}, f32[3,8,64,128]{3,2,1,0:T(8,128)}, u32[]{:S(2)}) %copy-start.1) | copy-done | bytes 786456
  3.7 0.0 copy-start.2
  3.7 0.9 %copy-done.2 = s32[8,64,128]{2,1,0:T(8,128)S(1)} copy-done((s32[8,64,128]{2,1,0:T(8,128)S(1)}, s32[8,64,128]{2,1,0:T(8,128)}, u32[]{:S(2)}) %copy-start.2) | copy-done | bytes 262168
  4.7 30.7 %shard_map.85 = (f32[3,8,64,128]{3,2,1,0:T(8,128)S(1)}, f32[3,8,64,128]{3,2,1,0:T(8,128)S(1)}, f32[8,4]{1,0:T(8,128)S(1)}) custom-call(f32[6]{0:T(128)S(1)} %copy-done.3, f32[6]{0:T(128)S(1)} %copy-done.4, s32[64,2]{1,0:T(8,128)S(1)} %copy.9.orders_ref, f32[3,8,64,128]{3,2,1,0:T(8,128)S(1)} %copy-done, f32[3,8,64,128]{3,2,1,0:T(8,128)S(1)} %copy-done.1, ...), custom_call_target="tpu_custom_call" | custom-call | tf_op jit(solution)/shard_map/pallas_call | solution.py:353
  35.4 0.7 %copy.10 = f32[8,4]{0,1:T(4,128)} copy(f32[8,4]{1,0:T(8,128)S(1)} %get-tuple-element.5) | data formatting | bytes 256 | tf_op jit(solution)/shard_map/pallas_call | solution.py:353
  36.0 0.9 %copy.13 = f32[3,8,64,128]{3,2,1,0:T(8,128)} copy(f32[3,8,64,128]{3,2,1,0:T(8,128)S(1)} %get-tuple-element.9) | data formatting | bytes 1572864
  36.9 0.9 %copy.14 = f32[3,8,64,128]{3,2,1,0:T(8,128)} copy(f32[3,8,64,128]{3,2,1,0:T(8,128)S(1)} %get-tuple-element.10) | data formatting | bytes 1572864
Async XLA Ops:
  0.6 0.8 %copy-start.4 = (f32[6]{0:T(128)S(1)}, f32[6]{0:T(128)}, u32[]{:S(2)}) copy-start(f32[6]{0:T(128)} %sigma_ref.1) | copy-start | bytes 76
  0.6 0.8 %copy-start.3 = (f32[6]{0:T(128)S(1)}, f32[6]{0:T(128)}, u32[]{:S(2)}) copy-start(f32[6]{0:T(128)} %eps_ref.1) | copy-start | bytes 76
  1.4 1.1 %copy-start = (f32[3,8,64,128]{3,2,1,0:T(8,128)S(1)}, f32[3,8,64,128]{3,2,1,0:T(8,128)}, u32[]{:S(2)}) copy-start(f32[3,8,64,128]{3,2,1,0:T(8,128)} %e_in.1) | copy-start | bytes 2359300
  2.6 1.1 %copy-start.1 = (f32[3,8,64,128]{3,2,1,0:T(8,128)S(1)}, f32[3,8,64,128]{3,2,1,0:T(8,128)}, u32[]{:S(2)}) copy-start(f32[3,8,64,128]{3,2,1,0:T(8,128)} %h_in.1) | copy-start | bytes 2359300
  3.7 0.9 %copy-start.2 = (s32[8,64,128]{2,1,0:T(8,128)S(1)}, s32[8,64,128]{2,1,0:T(8,128)}, u32[]{:S(2)}) copy-start(s32[8,64,128]{2,1,0:T(8,128)} %mat_in.1) | copy-start | bytes 786436

commit v2 on v1

--- a/solution.py
+++ b/solution.py
@@ -22,7 +22,7 @@
     size_x, size_y,
     eps_ref, sigma_ref, orders_ref, e_in, h_in, mat_in,
     e_out, h_out, far_ref,
-    elec, magn, mat, coef, mon, tables,
+    elec, magn, mat, coef, mon, table_y, table_x,
     fwd_send, fwd_recv, back_send, back_recv,
     rowe_send, rowe_recv, rowh_send, rowh_recv,
     core_send, core_recv, corh_send, corh_recv,
@@ -52,9 +52,9 @@
     hbody = pl.ds(PAD, cells_y)
     edge_e = load(e_in.at[:, last], elec.at[:, last, ebody], 0)
     edge_h = load(h_in.at[:, last], magn.at[:, last, hbody], 1)
-    rest_e = load(e_in.at[:, inner], elec.at[:, inner, ebody], 2)
-    rest_h = load(h_in.at[:, inner], magn.at[:, inner, hbody], 3)
-    load_mat = load(mat_in, mat, 4)
+    rest_e = [load(e_in.at[c, inner], elec.at[c, inner, ebody], 2 + c) for c in range(3)]
+    rest_h = [load(h_in.at[c, inner], magn.at[c, inner, hbody], 5 + c) for c in range(3)]
+    load_mat = load(mat_in, mat, 8)
 
     def member(offset):
         index = lax.rem(me + offset, group)
@@ -103,8 +103,8 @@
     def corh_copy(k):
         return copy_to(k, CORNER_H, corh_send.at[k], corh_recv.at[k], left, above)
 
-    def magn_plane(x, ahead, stage=None):
-        for r in starts:
+    def magn_plane(x, ahead, stage=None, parts=starts):
+        for r in parts:
             rows, upper, hrows = pl.ds(r, chunk), pl.ds(r + 1, chunk), pl.ds(PAD + r, chunk)
             ex, ey, ez = elec[0, x, rows], elec[1, x, rows], elec[2, x, rows]
             dyx = elec[0, x, upper] - ex
@@ -167,15 +167,18 @@
         core_copy(k).start()
 
     mon[...] = jnp.zeros_like(mon)
+    terms_send[...] = jnp.zeros_like(terms_send)
     edge_e.wait()
     edge_h.wait()
     magn_plane(last, None, 0)
     pl.semaphore_wait(barrier, group - 1)
     back_copy(0).start()
     send_fwd(0)
-    rest_e.wait()
+    for copy in rest_e:
+        copy.wait()
     send_back(0)
-    rest_h.wait()
+    for copy in rest_h:
+        copy.wait()
 
     row63 = pl.ds(PAD + cells_y - 1, 1)
     halo = pl.ds(PAD - 1, 1)
@@ -189,17 +192,16 @@
         stores.append(copy)
 
     for k in range(ITERS):
-        def magn_body(x, carry):
-            magn_plane(x, x + 1)
-            return carry
-
-        lax.fori_loop(0, last, magn_body, 0)
         rowe_send[k, 0] = elec[0, :, row0]
         rowe_send[k, 1] = elec[2, :, row0]
+        rowe_copy(k).start()
+        for x in range(last):
+            magn_plane(x, x + 1, parts=starts[-1:])
         rowh_send[k, 0] = magn[0, :, row63]
         rowh_send[k, 1] = magn[2, :, row63]
-        rowe_copy(k).start()
         rowh_copy(k).start()
+        for x in range(last):
+            magn_plane(x, x + 1, parts=starts[:-1])
         if k == 0:
             load_mat.wait()
             count = eps_ref.shape[0]
@@ -226,17 +228,18 @@
 
             lax.fori_loop(0, cells_x, coef_body, 0)
         if k == 1:
-            shape = (orders_ref.shape[0], depth)
-            wide = lax.broadcasted_iota(jnp.int32, shape, 1)
-            for slot, axis, pos, extent in (
-                (0, 1, me_y * cells_y + wide, size_y * cells_y),
-                (2, 0, me_x * cells_x + lax.rem(wide, cells_x), size_x * cells_x),
-            ):
-                order = jnp.broadcast_to(orders_ref[:, axis:axis + 1], shape)
-                turns = (order * pos).astype(jnp.float32) * (1.0 / extent)
+            orders = jnp.concatenate([orders_ref[...], orders_ref[...]], axis=1)
+            for table, axis, extent in ((table_y, 1, size_y * cells_y), (table_x, 0, size_x * cells_x)):
+                shape = table.shape
+                pos = lax.broadcasted_iota(jnp.int32, shape, 0)
+                if axis == 1:
+                    pos = me_y * cells_y + pos
+                else:
+                    pos = me_x * cells_x + lax.rem(pos, cells_x)
+                turns = (jnp.broadcast_to(orders[axis:axis + 1], shape) * pos).astype(jnp.float32) * (1.0 / extent)
                 angle = (turns - jnp.floor(turns)) * (2.0 * math.pi)
-                tables[slot] = jnp.cos(angle)
-                tables[slot + 1] = jnp.sin(angle)
+                wide = lax.broadcasted_iota(jnp.int32, shape, 1)
+                table[...] = jnp.where(wide < shape[1] // 2, jnp.cos(angle), jnp.sin(angle))
 
         rowe_copy(k).wait_recv()
         rowh_copy(k).wait_recv()
@@ -245,11 +248,8 @@
         magn[0, :, halo] = rowh_recv[k, 0] - TIME_STEP * elec[2, :, row0]
         magn[2, :, halo] = rowh_recv[k, 1] + TIME_STEP * elec[0, :, row0]
 
-        def elec_body(x, carry):
+        for x in range(1, last):
             elec_plane(x, local_previous(x), k + 1)
-            return carry
-
-        lax.fori_loop(1, last, elec_body, 0)
         final = k == ITERS - 1
         if final:
             store(magn.at[:, inner, hbody], h_out.at[:, inner])
@@ -287,46 +287,43 @@
             store(elec.at[:, last, ebody], e_out.at[:, last])
 
     span = 2 * cells_x
-    total = mon[...]
-    by_cos = jnp.dot(tables[0, :, pl.ds(0, cells_y)], total, precision=HIGH, preferred_element_type=jnp.float32)
-    by_sin = jnp.dot(tables[1, :, pl.ds(0, cells_y)], total, precision=HIGH, preferred_element_type=jnp.float32)
-    part_re = by_cos + pltpu.roll(by_sin, depth - span, 1)
-    part_im = pltpu.roll(by_cos, depth - span, 1) - by_sin
-    cos_x, sin_x = tables[2], tables[3]
-    wide = lax.broadcasted_iota(jnp.int32, part_re.shape, 1)
-    real = jnp.where(wide < span, cos_x * part_re + sin_x * part_im, 0.0)
-    imag = jnp.where(wide < span, cos_x * part_im - sin_x * part_re, 0.0)
-    both = real + pltpu.roll(imag, span, 1)
-    owned = terms_send.shape[1]
-    for peer in range(size_x):
-        terms_send[peer] = both[peer * owned:(peer + 1) * owned]
+    total = jnp.transpose(mon[...])[:2 * span]
+    by_cos = jnp.dot(total, table_y[...], precision=HIGH, preferred_element_type=jnp.float32)
+    angles = by_cos.shape[1] // 2
+    by_sin = pltpu.roll(by_cos, angles, 1)
+    part_re = by_cos[:span] + by_sin[span:]
+    part_im = by_cos[span:] - by_sin[:span]
+    cos_x = table_x[...]
+    sin_x = pltpu.roll(cos_x, angles, 1)
+    real = cos_x * part_re + sin_x * part_im
+    imag = cos_x * part_im - sin_x * part_re
+    for row, value in enumerate((real[:cells_x], imag[:cells_x], real[cells_x:], imag[cells_x:])):
+        terms_send[row:row + 1] = jnp.sum(value, axis=0, keepdims=True)
 
     def far_copy(offset):
         tx, ty = member(offset)
         return pltpu.make_async_remote_copy(
-            src_ref=terms_send.at[tx], dst_ref=terms_recv.at[me],
+            src_ref=terms_send, dst_ref=terms_recv.at[me],
             send_sem=far_send_sem.at[offset], recv_sem=far_recv_sem.at[me],
             device_id={"gx": tx, "gy": ty}, device_id_type=MESH,
         )
 
     for offset in range(1, group):
         far_copy(offset).start()
-    answer = terms_send[me_x]
+    answer = terms_send[...]
     for offset in range(1, group):
         source = lax.rem(me + offset, group)
         pltpu.make_async_remote_copy(
-            src_ref=terms_send.at[0], dst_ref=terms_recv.at[source],
+            src_ref=terms_send, dst_ref=terms_recv.at[source],
             send_sem=far_send_sem.at[offset], recv_sem=far_recv_sem.at[source],
             device_id={"gx": right, "gy": me_y}, device_id_type=MESH,
         ).wait_recv()
         answer = answer + terms_recv[source]
-    source_lane = lax.broadcasted_iota(jnp.int32, (depth, depth), 0) // cells_x
-    target_lane = lax.broadcasted_iota(jnp.int32, (depth, depth), 1)
-    picked = jnp.where(source_lane < 2, 2 * source_lane, 2 * source_lane - 3)
-    pick = jnp.where((source_lane < 4) & (picked == target_lane), 1.0, 0.0)
-    summed = jnp.dot(answer, pick, precision=HIGH, preferred_element_type=jnp.float32)
+    owned = far_ref.shape[1]
+    width = answer.shape[1]
+    mine = pltpu.roll(answer, lax.rem(width - owned * me_x, width), 1)
     scale = 1.0 / math.sqrt(size_x * cells_x * size_y * cells_y)
-    far_ref[...] = summed[:, :4] * scale
+    far_ref[...] = mine[:4, :owned] * scale
 
     for copy in stores:
         copy.wait()
@@ -345,38 +342,40 @@
     f32 = jnp.float32
     vmem = functools.partial(pl.BlockSpec, memory_space=pltpu.VMEM)
     smem = functools.partial(pl.BlockSpec, memory_space=pltpu.SMEM)
-    hbm = functools.partial(pl.BlockSpec, memory_space=pl.ANY)
+    hbm = functools.partial(pl.BlockSpec, memory_space=pltpu.HBM)
     dma = pltpu.SemaphoreType.DMA
     planes = pltpu.VMEM((ITERS, 2, cells_y, depth), f32)
     rows = pltpu.VMEM((ITERS, 2, cells_x, 1, depth), f32)
     corner = pltpu.VMEM((ITERS, 8, depth), f32)
-    return pl.pallas_call(
+    elec, magn, far = pl.pallas_call(
         functools.partial(kernel, size_x, size_y),
         out_shape=(
             jax.ShapeDtypeStruct(e_field.shape, f32),
             jax.ShapeDtypeStruct(h_field.shape, f32),
-            jax.ShapeDtypeStruct((owned, 4), f32),
+            jax.ShapeDtypeStruct((4, owned), f32),
         ),
         in_specs=[smem(), smem(), vmem(), hbm(), hbm(), hbm()],
-        out_specs=(hbm(), hbm(), vmem()),
+        out_specs=(pl.BlockSpec(memory_space=pl.ANY), pl.BlockSpec(memory_space=pl.ANY), vmem()),
         scratch_shapes=[
             pltpu.VMEM((3, cells_x, cells_y + PAD, depth), f32),
             pltpu.VMEM((3, cells_x, cells_y + PAD, depth), f32),
             pltpu.VMEM((cells_x, cells_y, depth), jnp.int32),
             pltpu.VMEM((2, cells_x, cells_y, depth), f32),
             pltpu.VMEM((cells_y, depth), f32),
-            pltpu.VMEM((4, angles, depth), f32),
+            pltpu.VMEM((cells_y, 2 * angles), f32),
+            pltpu.VMEM((2 * cells_x, 2 * angles), f32),
             planes, planes, planes, planes,
             rows, rows, rows, rows,
             corner, corner, corner, corner,
-            pltpu.VMEM((size_x, owned, depth), f32),
-            pltpu.VMEM((group, owned, depth), f32),
-            dma((5,)), dma((5,)), dma((ITERS, 6)), dma((ITERS, 6)), dma((group,)), dma((group,)),
+            pltpu.VMEM((8, 2 * angles), f32),
+            pltpu.VMEM((group, 8, 2 * angles), f32),
+            dma((9,)), dma((5,)), dma((ITERS, 6)), dma((ITERS, 6)), dma((group,)), dma((group,)),
         ],
         compiler_params=pltpu.CompilerParams(
-            collective_id=0, has_side_effects=True, vmem_limit_bytes=32 * 1024 * 1024
+            collective_id=0, has_side_effects=True, vmem_limit_bytes=60 * 1024 * 1024
         ),
-    )(eps_table, sigma_table, angle_orders, e_field, h_field, material)
+    )(eps_table, sigma_table, angle_orders.T, e_field, h_field, material)
+    return elec, magn, far.T
 
 
 def solution(mesh):

time: 38 us -> 35.9 us (0.945)
  local copies, waits for them, and re-layouts: 6.41 us -> 3.63 us
  Pallas kernels: 30.7 us -> 31.5 us
    unnamed x13 -> x7, local copies, waits for them, and re-layouts: 5.76 us -> 3.63 us
    pallas_call x1, Pallas kernels: 30.7 us -> 31.5 us  [local(): pl.pallas_call(functools.partial(kernel, size_x, size_y), out_shape=(jax....]
    pallas_call x1 -> x0, local copies, waits for them, and re-layouts: 0.65 us -> none  [local(): pl.pallas_call(functools.partial(kernel, size_x, size_y), out_shape=(jax....]
where the time goes in v2:
time: 35.9 us; the launch traced here: 35.7 us
  Pallas kernels  31.5 us (88%)
  local copies, waits for them, and re-layouts  3.63 us (10%)
  between operations  0.65 us (2%)
    pallas_call x1, Pallas kernels, local(): pl.pallas_call(functools.partial(kernel, size_x, size_y), out_shape=(jax....  31.5 us
    unnamed x7, local copies, waits for them, and re-layouts  3.63 us

profile of v2, /device:TPU:0, one launch (start us, length us, event | category | flops | bytes accessed | tf_op | source)
XLA Modules:
  0.0 35.7 jit_solution(12180514577721445074)
XLA Ops:
  0.6 31.5 %shard_map.85 = (f32[3,8,64,128]{3,2,1,0:T(8,128)}, f32[3,8,64,128]{3,2,1,0:T(8,128)}, f32[4,8]{1,0:T(4,128)}) custom-call(f32[6]{0:T(128)} %eps_ref.1, f32[6]{0:T(128)} %sigma_ref.1, s32[2,64]{1,0:T(2,128)} %bitcast.3, f32[3,8,64,128]{3,2,1,0:T(8,128)} %e_in.1, f32[3,8,64,128]{3,2,1,0:T(8,128)} %h_in.1, s32[8,64,128]{2,1,0:T(8,128)} %mat_in.1), custom_call_target="tpu_custom_call" | custom-call | tf_op jit(solution)/shard_map/pallas_call | solution.py:350
  32.1 0.0 copy-start
  32.1 2.2 %copy.12 = f32[3,8,64,128]{3,2,1,0:T(8,128)} copy(f32[3,8,64,128]{3,2,1,0:T(8,128)} %get-tuple-element.12) | data formatting | bytes 1572864
  34.3 0.0 copy-done
  34.3 0.0 copy-start.1
  34.3 0.9 %copy.13 = f32[3,8,64,128]{3,2,1,0:T(8,128)} copy(f32[3,8,64,128]{3,2,1,0:T(8,128)S(1)} %copy-done) | data formatting | bytes 1572864
  35.1 0.0 copy-done.1
  35.1 0.6 %copy.14 = f32[8,4]{0,1:T(4,128)} copy(f32[8,4]{0,1:T(4,128)S(1)} %bitcast.2) | data formatting | bytes 256
Async XLA Ops:
  32.1 2.2 %copy-start = (f32[3,8,64,128]{3,2,1,0:T(8,128)S(1)}, f32[3,8,64,128]{3,2,1,0:T(8,128)}, u32[]{:S(2)}) copy-start(f32[3,8,64,128]{3,2,1,0:T(8,128)} %get-tuple-element.13) | copy-start | bytes 2359300
  34.3 0.9 %copy-start.1 = (f32[4,8]{1,0:T(4,128)S(1)}, f32[4,8]{1,0:T(4,128)}, u32[]{:S(2)}) copy-start(f32[4,8]{1,0:T(4,128)} %get-tuple-element.8) | copy-start | bytes 388

commit v3 on v2

--- a/solution.py
+++ b/solution.py
@@ -15,7 +15,17 @@
 PAD = 8
 HIGH = lax.Precision.HIGHEST
 
-FWD, BACK, ROW_E, ROW_H, CORNER_E, CORNER_H = range(6)
+FWD, BACK, ROW_E, ROW_H, CORNER_E, CORNER_H = 0, 3, 6, 7, 8, 9
+
+
+def split(low, high):
+    return [(r, min(32, high - r)) for r in range(low, high, 32)]
+
+
+def edge_pieces(cells_y):
+    big, mid, small = 3 * cells_y // 4, 5 * cells_y // 8, cells_y // 2
+    first = ((0, big), (0, mid), (8, mid), (8, small))
+    return [((low, high), (high, cells_y)) + (((0, low),) if low else ()) for low, high in first]
 
 
 def kernel(
@@ -32,7 +42,8 @@
     cells_x, cells_y, depth = mat.shape
     last = cells_x - 1
     chunk = min(32, cells_y)
-    starts = range(0, cells_y, chunk)
+    starts = [(r, chunk) for r in range(0, cells_y, chunk)]
+    pieces = edge_pieces(cells_y)
     me_x = lax.axis_index("gx")
     me_y = lax.axis_index("gy")
     right = lax.rem(me_x + 1, size_x)
@@ -65,15 +76,14 @@
         tx, ty = member(offset)
         pl.semaphore_signal(barrier, inc=1, device_id={"gx": tx, "gy": ty}, device_id_type=MESH)
 
-    lane = lax.broadcasted_iota(jnp.int32, (chunk, depth), 1)
-    first_lane = lane == 0
-    last_lane = lane == depth - 1
+    def lanes(size):
+        return lax.broadcasted_iota(jnp.int32, (size, depth), 1)
 
     def forward_z(value):
-        return jnp.where(last_lane, 0.0, pltpu.roll(value, depth - 1, 1)) - value
+        return jnp.where(lanes(value.shape[0]) == depth - 1, 0.0, pltpu.roll(value, depth - 1, 1)) - value
 
     def backward_z(value):
-        return value - jnp.where(first_lane, 0.0, pltpu.roll(value, 1, 1))
+        return value - jnp.where(lanes(value.shape[0]) == 0, 0.0, pltpu.roll(value, 1, 1))
 
     elec[:, :, pl.ds(cells_y, PAD), :] = jnp.zeros((3, cells_x, PAD, depth), jnp.float32)
 
@@ -84,12 +94,18 @@
             device_id={"gx": tx, "gy": ty}, device_id_type=MESH,
         )
 
-    def fwd_copy(k):
-        return copy_to(k, FWD, fwd_send.at[k], fwd_recv.at[k], right, me_y)
-
-    def back_copy(k):
-        src = e_in.at[pl.ds(1, 2), 0] if k == 0 else back_send.at[k]
-        return copy_to(k, BACK, src, back_recv.at[k], left, me_y)
+    def piece_rows(k, piece):
+        low, high = pieces[k][piece]
+        return pl.ds(low, high - low)
+
+    def fwd_copy(k, piece):
+        rows = piece_rows(k, piece)
+        return copy_to(k, FWD + piece, fwd_send.at[k, :, rows], fwd_recv.at[k, :, rows], right, me_y)
+
+    def back_copy(k, piece):
+        rows = piece_rows(max(k - 1, 0), piece)
+        src = e_in.at[pl.ds(1, 2), 0, rows] if k == 0 else back_send.at[k, :, rows]
+        return copy_to(k, BACK + piece, src, back_recv.at[k, :, rows], left, me_y)
 
     def rowe_copy(k):
         return copy_to(k, ROW_E, rowe_send.at[k], rowe_recv.at[k], me_x, below)
@@ -104,8 +120,8 @@
         return copy_to(k, CORNER_H, corh_send.at[k], corh_recv.at[k], left, above)
 
     def magn_plane(x, ahead, stage=None, parts=starts):
-        for r in parts:
-            rows, upper, hrows = pl.ds(r, chunk), pl.ds(r + 1, chunk), pl.ds(PAD + r, chunk)
+        for r, size in parts:
+            rows, upper, hrows = pl.ds(r, size), pl.ds(r + 1, size), pl.ds(PAD + r, size)
             ex, ey, ez = elec[0, x, rows], elec[1, x, rows], elec[2, x, rows]
             dyx = elec[0, x, upper] - ex
             dyz = elec[2, x, upper] - ez
@@ -122,14 +138,15 @@
                 fwd_send[stage, 0, rows] = hy
                 fwd_send[stage, 1, rows] = hz
 
-    def elec_plane(x, previous, number, stage=None):
+    def elec_plane(x, previous, number, stage=None, parts=starts):
         cos_n = math.cos(PHASE_STEP * number)
         sin_n = math.sin(PHASE_STEP * number)
-        for r in starts:
-            rows, hrows, lower = pl.ds(r, chunk), pl.ds(PAD + r, chunk), pl.ds(PAD + r - 1, chunk)
+        for r, size in parts:
+            rows, hrows, lower = pl.ds(r, size), pl.ds(PAD + r, size), pl.ds(PAD + r - 1, size)
+            lane = lanes(size)
             hx, hy, hz = magn[0, x, hrows], magn[1, x, hrows], magn[2, x, hrows]
             ex, ey, ez = elec[0, x, rows], elec[1, x, rows], elec[2, x, rows]
-            prev_y, prev_z = previous(r, ey, ez)
+            prev_y, prev_z = previous(r, size, ey, ez)
             keep, drive = coef[0, x, rows], coef[1, x, rows]
             new_x = keep * ex + drive * ((hz - magn[2, x, lower]) - backward_z(hy))
             new_y = keep * ey + drive * (backward_z(hx) - (hz - prev_z))
@@ -144,26 +161,21 @@
             for comp, new in ((0, new_x), (1, new_y)):
                 slot = comp * cells_x + x
                 weight = jnp.where(lane == slot, cos_n, jnp.where(lane == slot + 2 * cells_x, -sin_n, 0.0))
-                total = total + jnp.broadcast_to(new[:, depth - 3:depth - 2], (chunk, depth)) * weight
+                total = total + jnp.broadcast_to(new[:, depth - 3:depth - 2], (size, depth)) * weight
             mon[rows] = total
 
     def local_previous(x):
-        def previous(r, ey, ez):
-            hrows = pl.ds(PAD + r, chunk)
+        def previous(r, size, ey, ez):
+            hrows = pl.ds(PAD + r, size)
             return magn[1, x - 1, hrows], magn[2, x - 1, hrows]
         return previous
 
-    def send_back(k):
-        if k == 0:
-            corh_send[k] = elec[1, 0, pl.ds(cells_y - 8, 8)]
-        else:
-            corh_send[k] = back_send[k, 0, pl.ds(cells_y - 8, 8)]
-            back_copy(k).start()
+    def send_corner_h(k):
+        corh_send[k] = elec[1, 0, pl.ds(cells_y - 8, 8)]
         corh_copy(k).start()
 
-    def send_fwd(k):
+    def send_corner_e(k):
         core_send[k] = elec[0, last, pl.ds(0, 8)]
-        fwd_copy(k).start()
         core_copy(k).start()
 
     mon[...] = jnp.zeros_like(mon)
@@ -172,11 +184,13 @@
     edge_h.wait()
     magn_plane(last, None, 0)
     pl.semaphore_wait(barrier, group - 1)
-    back_copy(0).start()
-    send_fwd(0)
+    for piece in range(len(pieces[0])):
+        back_copy(0, piece).start()
+        fwd_copy(0, piece).start()
+    send_corner_e(0)
     for copy in rest_e:
         copy.wait()
-    send_back(0)
+    send_corner_h(0)
     for copy in rest_h:
         copy.wait()
 
@@ -214,7 +228,7 @@
                 drives.append((TIME_STEP / (permit * (1.0 + loss)))[:1])
 
             def coef_body(x, carry):
-                for r in starts:
+                for r, _ in starts:
                     rows = pl.ds(r, chunk)
                     ids = mat[x, rows]
                     keep = jnp.broadcast_to(keeps[0], (chunk, depth))
@@ -255,33 +269,72 @@
             store(magn.at[:, inner, hbody], h_out.at[:, inner])
             store(elec.at[:, pl.ds(1, last - 1), ebody], e_out.at[:, pl.ds(1, last - 1)])
 
-        fwd_copy(k).wait_recv()
-        core_copy(k).wait_recv()
-        fwd_recv[k, 1, pl.ds(cells_y - 1, 1)] = (
-            fwd_recv[k, 1, pl.ds(cells_y - 1, 1)] + TIME_STEP * core_recv[k, pl.ds(0, 1)]
-        )
-
-        def received(r, ey, ez):
-            rows = pl.ds(r, chunk)
+        def received(r, size, ey, ez):
+            rows = pl.ds(r, size)
             return fwd_recv[k, 0, rows] + TIME_STEP * ez, fwd_recv[k, 1, rows] - TIME_STEP * ey
 
-        elec_plane(0, received, k + 1, None if final else k + 1)
+        def first_plane(piece):
+            for at in ((0,) if piece == 0 else range(1, len(pieces[k]))):
+                fwd_copy(k, at).wait_recv()
+            if piece == 1:
+                core_copy(k).wait_recv()
+                fwd_recv[k, 1, pl.ds(cells_y - 1, 1)] = (
+                    fwd_recv[k, 1, pl.ds(cells_y - 1, 1)] + TIME_STEP * core_recv[k, pl.ds(0, 1)]
+                )
+            for at in ((0,) if piece == 0 else range(1, len(pieces[k]))):
+                elec_plane(0, received, k + 1, None if final else k + 1, split(*pieces[k][at]))
+                if not final:
+                    back_copy(k + 1, at).start()
+            if piece == 1 and not final:
+                send_corner_h(k + 1)
+
+        back_pieces = pieces[max(k - 1, 0)]
+
+        def add_ahead(low, high):
+            for r, size in split(low, high):
+                rows, hrows = pl.ds(r, size), pl.ds(PAD + r, size)
+                magn[1, last, hrows] = magn[1, last, hrows] + TIME_STEP * back_recv[k, 1, rows]
+                magn[2, last, hrows] = magn[2, last, hrows] - TIME_STEP * back_recv[k, 0, rows]
+
+        def last_halo():
+            corh_copy(k).wait_recv()
+            magn[2, last, halo] = magn[2, last, halo] - TIME_STEP * corh_recv[k, pl.ds(7, 1)]
+
+        def last_elec(low, high):
+            elec_plane(last, local_previous(last), k + 1, None, split(low, high))
+
+        def last_magn(low, high):
+            magn_plane(last, None, k + 1, split(low, high))
+
+        early_high = back_pieces[0][1]
+        early_low = back_pieces[0][0] + 8 if final else pieces[k + 1][0][0]
+
+        first_plane(0)
+        back_copy(k, 0).wait_recv()
+        add_ahead(*back_pieces[0])
+        if k == 0:
+            last_halo()
+        last_elec(early_low, early_high)
         if not final:
-            send_back(k + 1)
-        else:
+            low, high = pieces[k + 1][0]
+            last_magn(low, high)
+            fwd_copy(k + 1, 0).start()
+        first_plane(1)
+        if final:
             store(elec.at[:, 0, ebody], e_out.at[:, 0])
-
-        back_copy(k).wait_recv()
-        corh_copy(k).wait_recv()
-        for r in starts:
-            rows, hrows = pl.ds(r, chunk), pl.ds(PAD + r, chunk)
-            magn[1, last, hrows] = magn[1, last, hrows] + TIME_STEP * back_recv[k, 1, rows]
-            magn[2, last, hrows] = magn[2, last, hrows] - TIME_STEP * back_recv[k, 0, rows]
-        magn[2, last, halo] = magn[2, last, halo] - TIME_STEP * corh_recv[k, pl.ds(7, 1)]
-        elec_plane(last, local_previous(last), k + 1)
+        for at in range(1, len(back_pieces)):
+            back_copy(k, at).wait_recv()
+            add_ahead(*back_pieces[at])
+        if k > 0:
+            last_halo()
+        if early_low:
+            last_elec(0, early_low)
+        last_elec(early_high, cells_y)
         if not final:
-            magn_plane(last, None, k + 1)
-            send_fwd(k + 1)
+            for at in range(1, len(pieces[k + 1])):
+                last_magn(*pieces[k + 1][at])
+                fwd_copy(k + 1, at).start()
+            send_corner_e(k + 1)
         else:
             store(magn.at[:, last, hbody], h_out.at[:, last])
             store(elec.at[:, last, ebody], e_out.at[:, last])
@@ -328,10 +381,33 @@
     for copy in stores:
         copy.wait()
     for k in range(ITERS):
-        for copy in (fwd_copy, back_copy, rowe_copy, rowh_copy, core_copy, corh_copy):
+        for copy in (rowe_copy, rowh_copy, core_copy, corh_copy):
             copy(k).wait_send()
+        for piece in range(len(pieces[k])):
+            fwd_copy(k, piece).wait_send()
+        for piece in range(len(pieces[max(k - 1, 0)])):
+            back_copy(k, piece).wait_send()
     for offset in range(1, group):
         far_copy(offset).wait_send()
+
+
+def place(e_raw, h_raw, far_raw, e_out, h_out, far_out, e_held, h_held, far_held, in_sem, out_sem):
+    pairs = []
+    for x in range(0, e_raw.shape[1], 2):
+        planes = pl.ds(x, 2)
+        for c in range(3):
+            for raw, held, out in ((e_raw, e_held, e_out), (h_raw, h_held, h_out)):
+                pairs.append((raw.at[c, planes], held.at[c, planes], out.at[c, planes]))
+    pairs.append((far_raw, far_held, far_out))
+    loads = [pltpu.make_async_copy(raw, held, in_sem.at[i]) for i, (raw, held, _) in enumerate(pairs)]
+    saves = [pltpu.make_async_copy(held, out, out_sem.at[i]) for i, (_, held, out) in enumerate(pairs)]
+    for copy in loads:
+        copy.start()
+    for copy, save in zip(loads, saves):
+        copy.wait()
+        save.start()
+    for save in saves:
+        save.wait()
 
 
 def local(size_x, size_y, e_field, h_field, material, eps_table, sigma_table, angle_orders):
@@ -369,12 +445,23 @@
             corner, corner, corner, corner,
             pltpu.VMEM((8, 2 * angles), f32),
             pltpu.VMEM((group, 8, 2 * angles), f32),
-            dma((9,)), dma((5,)), dma((ITERS, 6)), dma((ITERS, 6)), dma((group,)), dma((group,)),
+            dma((9,)), dma((5,)), dma((ITERS, 10)), dma((ITERS, 10)), dma((group,)), dma((group,)),
         ],
         compiler_params=pltpu.CompilerParams(
             collective_id=0, has_side_effects=True, vmem_limit_bytes=60 * 1024 * 1024
         ),
     )(eps_table, sigma_table, angle_orders.T, e_field, h_field, material)
+    elec, magn, far = pl.pallas_call(
+        place,
+        out_shape=tuple(jax.ShapeDtypeStruct(value.shape, f32) for value in (elec, magn, far)),
+        in_specs=[hbm()] * 3,
+        out_specs=(hbm(),) * 3,
+        scratch_shapes=[
+            pltpu.VMEM(elec.shape, f32), pltpu.VMEM(magn.shape, f32), pltpu.VMEM(far.shape, f32),
+            dma((3 * cells_x + 1,)), dma((3 * cells_x + 1,)),
+        ],
+        compiler_params=pltpu.CompilerParams(vmem_limit_bytes=60 * 1024 * 1024),
+    )(elec, magn, far)
     return elec, magn, far.T
 
 

time: 35.9 us -> 34.3 us (0.955)
  local copies, waits for them, and re-layouts: 3.63 us -> 0 us
  Pallas kernels: 31.5 us -> 33.4 us
    unnamed x7 -> x0, local copies, waits for them, and re-layouts: 3.63 us -> none
    pallas_call x0 -> x1, Pallas kernels: none -> 2.49 us  [local(): pl.pallas_call(place, out_shape=tuple((jax.ShapeDtypeStruct(value.shape,...]
    pallas_call x1, Pallas kernels: 31.5 us -> 30.9 us  [local(): pl.pallas_call(functools.partial(kernel, size_x, size_y), out_shape=(jax....]
where the time goes in v3:
time: 34.3 us; the launch traced here: 34.1 us
  Pallas kernels  33.4 us (97%)
  between operations  0.64 us (2%)
    pallas_call x1, Pallas kernels, local(): pl.pallas_call(functools.partial(kernel, size_x, size_y), out_shape=(jax....  30.9 us
    pallas_call x1, Pallas kernels, local(): pl.pallas_call(place, out_shape=tuple((jax.ShapeDtypeStruct(value.shape,...  2.49 us

profile of v3, /device:TPU:0, one launch (start us, length us, event | category | flops | bytes accessed | tf_op | source)
XLA Modules:
  0.0 34.1 jit_solution(5037801826390076954)
XLA Ops:
  0.6 30.9 %shard_map.85 = (f32[3,8,64,128]{3,2,1,0:T(8,128)}, f32[3,8,64,128]{3,2,1,0:T(8,128)}, f32[4,8]{1,0:T(4,128)}) custom-call(f32[6]{0:T(128)} %eps_ref.1, f32[6]{0:T(128)} %sigma_ref.1, s32[2,64]{1,0:T(2,128)} %bitcast.2, f32[3,8,64,128]{3,2,1,0:T(8,128)} %e_in.1, f32[3,8,64,128]{3,2,1,0:T(8,128)} %h_in.1, s32[8,64,128]{2,1,0:T(8,128)} %mat_in.1), custom_call_target="tpu_custom_call" | custom-call | tf_op jit(solution)/shard_map/pallas_call | solution.py:426
  31.6 2.5 %shard_map.86 = (f32[3,8,64,128]{3,2,1,0:T(8,128)}, f32[3,8,64,128]{3,2,1,0:T(8,128)}, f32[4,8]{1,0:T(4,128)}) custom-call(f32[3,8,64,128]{3,2,1,0:T(8,128)} %get-tuple-element.9.e_raw, f32[3,8,64,128]{3,2,1,0:T(8,128)} %get-tuple-element.10.h_raw, f32[4,8]{1,0:T(4,128)} %get-tuple-element.11.far_raw), custom_call_target="tpu_custom_call" | custom-call | tf_op jit(solution)/shard_map/pallas_call | solution.py:454

commit v4 on v3

--- a/solution.py
+++ b/solution.py
@@ -393,11 +393,9 @@
 
 def place(e_raw, h_raw, far_raw, e_out, h_out, far_out, e_held, h_held, far_held, in_sem, out_sem):
     pairs = []
-    for x in range(0, e_raw.shape[1], 2):
-        planes = pl.ds(x, 2)
-        for c in range(3):
-            for raw, held, out in ((e_raw, e_held, e_out), (h_raw, h_held, h_out)):
-                pairs.append((raw.at[c, planes], held.at[c, planes], out.at[c, planes]))
+    for c in range(e_raw.shape[0]):
+        for raw, held, out in ((e_raw, e_held, e_out), (h_raw, h_held, h_out)):
+            pairs.append((raw.at[c], held.at[c], out.at[c]))
     pairs.append((far_raw, far_held, far_out))
     loads = [pltpu.make_async_copy(raw, held, in_sem.at[i]) for i, (raw, held, _) in enumerate(pairs)]
     saves = [pltpu.make_async_copy(held, out, out_sem.at[i]) for i, (_, held, out) in enumerate(pairs)]
@@ -458,7 +456,7 @@
         out_specs=(hbm(),) * 3,
         scratch_shapes=[
             pltpu.VMEM(elec.shape, f32), pltpu.VMEM(magn.shape, f32), pltpu.VMEM(far.shape, f32),
-            dma((3 * cells_x + 1,)), dma((3 * cells_x + 1,)),
+            dma((7,)), dma((7,)),
         ],
         compiler_params=pltpu.CompilerParams(vmem_limit_bytes=60 * 1024 * 1024),
     )(elec, magn, far)

time: 34.3 us -> 34 us (level)
  no operation moved by 1% of the time
where the time goes in v4:
time: 34 us; the launch traced here: 33.8 us
  Pallas kernels  33.1 us (97%)
  between operations  0.64 us (2%)
    pallas_call x1, Pallas kernels, local(): pl.pallas_call(functools.partial(kernel, size_x, size_y), out_shape=(jax....  30.9 us
    pallas_call x1, Pallas kernels, local(): pl.pallas_call(place, out_shape=tuple((jax.ShapeDtypeStruct(value.shape,...  2.21 us

profile of v4, /device:TPU:0, one launch (start us, length us, event | category | flops | bytes accessed | tf_op | source)
XLA Modules:
  0.0 33.8 jit_solution(10163194136730037133)
XLA Ops:
  0.6 30.9 %shard_map.85 = (f32[3,8,64,128]{3,2,1,0:T(8,128)}, f32[3,8,64,128]{3,2,1,0:T(8,128)}, f32[4,8]{1,0:T(4,128)}) custom-call(f32[6]{0:T(128)} %eps_ref.1, f32[6]{0:T(128)} %sigma_ref.1, s32[2,64]{1,0:T(2,128)} %bitcast.2, f32[3,8,64,128]{3,2,1,0:T(8,128)} %e_in.1, f32[3,8,64,128]{3,2,1,0:T(8,128)} %h_in.1, s32[8,64,128]{2,1,0:T(8,128)} %mat_in.1), custom_call_target="tpu_custom_call" | custom-call | tf_op jit(solution)/shard_map/pallas_call | solution.py:424
  31.6 2.2 %shard_map.86 = (f32[3,8,64,128]{3,2,1,0:T(8,128)}, f32[3,8,64,128]{3,2,1,0:T(8,128)}, f32[4,8]{1,0:T(4,128)}) custom-call(f32[3,8,64,128]{3,2,1,0:T(8,128)} %get-tuple-element.9.e_raw, f32[3,8,64,128]{3,2,1,0:T(8,128)} %get-tuple-element.10.h_raw, f32[4,8]{1,0:T(4,128)} %get-tuple-element.11.far_raw), custom_call_target="tpu_custom_call" | custom-call | tf_op jit(solution)/shard_map/pallas_call | solution.py:452
